TPU v7x, 32 devices: a whole 2x2x4 slice. The times are simulated.
32 devices in a mesh: dp: 8 (over y, x, core), context: 4 (over z).
Axes of the slice: x: 2, y: 2, z: 4, core: 2. Of those that a mesh axis runs over, the one named last changes fastest.
Arguments:
- residual_in: bfloat16 [8, 512, 4096], P('dp', 'context'), may hold values from -6 to 6
- residual_tangent: bfloat16 [8, 512, 4096], P('dp', 'context'), may hold values from -6 to 6
- queries: bfloat16 [8, 512, 4096], P('dp', 'context'), may hold values from -32 to 32, as said below
- key_rows: bfloat16 [8, 512, 4096], P('dp', 'context'), may hold values from -8 to 8
- value_rows: bfloat16 [8, 512, 4096], P('dp', 'context'), may hold values from -6 to 6
- query_tangent: bfloat16 [8, 512, 4096], P('dp', 'context'), may hold values from -6 to 6
- key_tangent: bfloat16 [8, 512, 4096], P('dp', 'context'), may hold values from -6 to 6
- value_tangent: bfloat16 [8, 512, 4096], P('dp', 'context'), may hold values from -6 to 6
- time_features: float32 [8, 4096], P('dp'), may hold values from -5 to 5
- time_tangent: float32 [8, 4096], P('dp'), may hold values from -5 to 5
- time_weight: bfloat16 [4096, 12288], P('dp', 'context'), may hold values from -0.09375 to 0.09375
- block_modulation: float32 [3, 4096], replicated, may hold values from -3 to 3
Outputs:
- normed: bfloat16 [8, 512, 4096], P('dp', 'context')
- normed_tangent: bfloat16 [8, 512, 4096], P('dp', 'context')
Inputs may be any that keep to these rules, and one draw needn't show every extreme that they name: `queries`: query entries.
All inputs are finite; a program needn't handle non-finite values.
Results may differ from a plain program's by a relative error of at most 0.0046.
Values may be sent and summed in bfloat16 or wider, within the bound.
A program may use at most 128 MiB of HBM per device.

v0:
```python
import jax
import jax.numpy as jnp
from jax import lax
from jax.sharding import PartitionSpec as P

HEADS = 32
HEAD = 128


def head_attention(query, keyset, values, query_dot, key_dot, value_dot):
    length = query.shape[0]
    size = min(512, length)
    count = length // size
    factor = 1.0 / query.shape[1] ** 0.5

    def one_block(pair):
        block_q, block_dq = pair
        scores = jnp.dot(block_q, keyset.T, preferred_element_type=jnp.float32) * factor
        score_dot = (
            jnp.dot(block_dq, keyset.T, preferred_element_type=jnp.float32)
            + jnp.dot(block_q, key_dot.T, preferred_element_type=jnp.float32)
        ) * factor
        top = jnp.max(scores, axis=1, keepdims=True)
        expo = jnp.exp(scores - top)
        probs = expo / jnp.sum(expo, axis=1, keepdims=True)
        probs_low = probs.astype(jnp.bfloat16)
        weighted = probs * score_dot
        centre = jnp.sum(weighted, axis=1, keepdims=True)
        weighted_low = weighted.astype(jnp.bfloat16)
        attended = jnp.dot(probs_low, values, preferred_element_type=jnp.float32)
        tangent = (
            jnp.dot(probs_low, value_dot, preferred_element_type=jnp.float32)
            + jnp.dot(weighted_low, values, preferred_element_type=jnp.float32)
            - centre * attended
        )
        return (attended.astype(jnp.bfloat16), tangent.astype(jnp.bfloat16))

    shaped = (query.reshape(count, size, -1), query_dot.reshape(count, size, -1))
    attended, tangent = lax.map(one_block, shaped)
    return (attended.reshape(length, -1), tangent.reshape(length, -1))


def prepare(resid, resid_dot, attended, attended_dot, mods, mods_dot):
    hidden_state = resid.astype(jnp.float32) + mods[0] * attended.astype(jnp.float32)
    hidden_tangent = (
        resid_dot.astype(jnp.float32)
        + mods[0] * attended_dot.astype(jnp.float32)
        + mods_dot[0] * attended.astype(jnp.float32)
    )
    centered = hidden_state - jnp.mean(hidden_state, axis=1, keepdims=True)
    inverse = lax.rsqrt(jnp.mean(centered * centered, axis=1, keepdims=True) + 1e-06)
    unit = centered * inverse
    unit_dot = (
        hidden_tangent
        - jnp.mean(hidden_tangent, axis=1, keepdims=True)
        - unit * jnp.mean(unit * hidden_tangent, axis=1, keepdims=True)
    ) * inverse
    normed = (unit * (1.0 + mods[2]) + mods[1]).astype(jnp.bfloat16)
    normed_dot = (unit_dot * (1.0 + mods[2]) + unit * mods_dot[2] + mods_dot[1]).astype(
        jnp.bfloat16
    )
    return (normed, normed_dot)


def time_modulation(time_features, time_tangent, time_weight, block_modulation):
    act, act_dot = jax.jvp(jax.nn.silu, (time_features,), (time_tangent,))
    both = jnp.stack([act.astype(jnp.bfloat16), act_dot.astype(jnp.bfloat16)])
    full_rows = lax.all_gather(time_weight, "dp", axis=0, tiled=True)
    local = jnp.einsum("bcd,de->bce", both, full_rows, preferred_element_type=jnp.float32)
    whole = lax.all_gather(local, "context", axis=2, tiled=True)
    width = time_features.shape[1]
    mods = block_modulation + whole[0, 0].reshape(3, width)
    mods_dot = whole[1, 0].reshape(3, width)
    return (mods, mods_dot)


def on_device(
    residual_in,
    residual_tangent,
    queries,
    key_rows,
    value_rows,
    query_tangent,
    key_tangent,
    value_tangent,
    time_features,
    time_tangent,
    time_weight,
    block_modulation,
):
    tokens_dev = residual_in.shape[1]
    width = residual_in.shape[2]
    sources = (queries, key_rows, value_rows, query_tangent, key_tangent, value_tangent)
    stacked = jnp.stack([source[0].reshape(tokens_dev, HEADS, HEAD) for source in sources])
    spread_out = lax.all_to_all(stacked, "context", split_axis=2, concat_axis=1, tiled=True)
    mods, mods_dot = time_modulation(time_features, time_tangent, time_weight, block_modulation)
    per_head = jnp.transpose(spread_out, (0, 2, 1, 3))
    attended, attended_dot = lax.map(
        lambda group: head_attention(*group), tuple((per_head[slot] for slot in range(6)))
    )
    joined = jnp.stack([attended, attended_dot])
    returned = lax.all_to_all(joined, "context", split_axis=2, concat_axis=1, tiled=True)
    merged = jnp.transpose(returned, (0, 2, 1, 3)).reshape(2, tokens_dev, width)
    normed, normed_dot = prepare(
        residual_in[0], residual_tangent[0], merged[0], merged[1], mods, mods_dot
    )
    return (normed[None], normed_dot[None])


def solution(mesh):
    return jax.shard_map(
        on_device,
        mesh=mesh,
        in_specs=(
            P("dp", "context", None),
            P("dp", "context", None),
            P("dp", "context", None),
            P("dp", "context", None),
            P("dp", "context", None),
            P("dp", "context", None),
            P("dp", "context", None),
            P("dp", "context", None),
            P("dp", None),
            P("dp", None),
            P("dp", "context"),
            P(),
        ),
        out_specs=(P("dp", "context", None), P("dp", "context", None)),
        check_vma=False,
    )
```

profile of v0, /device:TPU:0, one launch (start us, length us, event | category | flops | bytes accessed | tf_op | source)
XLA Modules:
  0.0 358.3 jit_solution(17329758391590718091)
XLA Ops:
  8.4 1.3 copy.52
  9.7 1.3 copy.53
  11.0 1.3 copy.54
  13.0 1.6 copy.56
  14.6 1.6 copy.57
  16.3 2.5 constant_dynamic-update-slice_fusion.5
  20.9 1.1 constant_dynamic-update-slice_fusion.2
  23.0 1.1 constant_dynamic-update-slice_fusion
  24.1 8.9 %copy.58 = bf16[6,128,32,128]{3,1,0,2:T(8,128)(2,1)} copy(bf16[6,128,32,128]{1,3,2,0:T(8,128)(2,1)} %constant_dynamic-update-slice_fusion) | data formatting | bytes 12582912 | tf_op jit(solution)/shard_map/stack | solution.py:94
  33.0 6.3 %all-to-all-start = ((bf16[6,128,32,128]{3,1,0,2:T(8,128)(2,1)}), bf16[6,128,32,128]{3,1,0,2:T(8,128)(2,1)}, u32[]{:S(2)}, u32[]{:S(2)}) async-start(bf16[6,128,32,128]{3,1,0,2:T(8,128)(2,1)} %copy.58), calls=%async_computation | async-start | bytes 12582912 | tf_op jit(solution)/shard_map/all_to_all | solution.py:95
  39.3 138.9 %all-to-all-done = bf16[6,128,32,128]{3,1,0,2:T(8,128)(2,1)} async-done(((bf16[6,128,32,128]{3,1,0,2:T(8,128)(2,1)}), bf16[6,128,32,128]{3,1,0,2:T(8,128)(2,1)}, u32[]{:S(2)}, u32[]{:S(2)}) %all-to-all-start) | async-done | bytes 6291488 | tf_op jit(solution)/shard_map/all_to_all | solution.py:95
  178.2 8.5 %copy.60 = bf16[6,4,128,8,128]{4,3,2,1,0:T(8,128)(2,1)S(1)} copy(bf16[6,4,128,8,128]{4,2,0,3,1:T(8,128)(2,1)} %bitcast.20) | data formatting | bytes 12582912 | tf_op jit(solution)/shard_map/all_to_all | solution.py:95
  187.2 1.2 copy.66
  188.3 1.2 copy.65
  189.5 1.1 copy.64
  190.9 1.2 copy.61
  192.1 59.4 %while.12 = (s32[]{:T(128)}, bf16[8,512,128]{2,1,0:T(8,128)(2,1)}, bf16[8,512,128]{2,1,0:T(8,128)(2,1)}, bf16[8,512,128]{2,1,0:T(8,128)(2,1)}, bf16[8,512,128]{2...) while((s32[]{:T(128)}, bf16[8,512,128]{2,1,0:T(8,128)(2,1)}, ...), condition=%wide.region_4.5_spmd, body=%wide.region_0.4_spmd.sunk | while | flops 406649344 | bytes 11426929 | solution.py:98
  192.1 1.2 fusion.94
  193.3 1.2 fusion.90
  194.8 1.4 fusion.95
  196.3 1.2 fusion.93
  199.6 1.2 fusion.94
  200.8 1.2 fusion.90
  202.2 1.4 fusion.95
  203.7 1.2 fusion.93
  207.0 1.2 fusion.94
  208.2 1.2 fusion.90
  209.6 1.4 fusion.95
  211.2 1.2 fusion.93
  214.4 1.2 fusion.94
  215.6 1.2 fusion.90
  217.0 1.4 fusion.95
  218.6 1.2 fusion.93
  221.9 1.2 fusion.94
  223.0 1.2 fusion.90
  224.5 1.4 fusion.95
  226.0 1.2 fusion.93
  229.3 1.2 fusion.94
  230.5 1.2 fusion.90
  231.9 1.4 fusion.95
  233.5 1.2 fusion.93
  236.7 1.2 fusion.94
  237.9 1.2 fusion.90
  239.3 1.4 fusion.95
  240.9 1.2 fusion.93
  244.1 1.2 fusion.94
  245.3 1.2 fusion.90
  246.7 1.4 fusion.95
  248.3 1.2 fusion.93
  251.6 2.9 copy_bitcast_fusion
  254.5 1.7 pad_maximum_fusion
  256.1 3.8 %all-to-all-start.1 = ((bf16[2,8,512,128]{3,1,0,2:T(8,128)(2,1)}), bf16[2,8,512,128]{3,1,0,2:T(8,128)(2,1)S(1)}, u32[]{:S(2)}, u32[]{:S(2)}) async-start(bf16[2,8,512,128]{3,1,0,2:T(8,128)(2,1)} %pad_maximum_fusion), calls=%async_computation.1 | async-start | bytes 4194304 | tf_op jit(solution)/shard_map/all_to_all | solution.py:102
  260.0 1.6 copy.51
  261.6 2.3 copy.73
  264.0 43.6 %all-to-all-done.1 = bf16[2,8,512,128]{3,1,0,2:T(8,128)(2,1)S(1)} async-done(((bf16[2,8,512,128]{3,1,0,2:T(8,128)(2,1)}), bf16[2,8,512,128]{3,1,0,2:T(8,128)(2,1)S(1)}, u32[]{:S(2)}, u32[]{:S(2)}) %all-to-all-start.1) | async-done | bytes 2097184 | tf_op jit(solution)/shard_map/all_to_all | solution.py:102
  308.2 1.8 slice_convert_fusion
  310.0 1.8 copy.74
  311.9 1.9 copy.71
  313.8 9.9 %fusion.55 = f32[2,3072]{1,0:T(2,128)S(1)} fusion(bf16[4096,3072]{1,0:T(8,128)(2,1)} %all-gather.3.cloned.1.call-done, bf16[1,1,4096]{2,0,1:T(2,128)(2,1)S(1)} %convert_bitcast_fusion.2, bf16[1,1,4096]{2,0,1:T(2,128)(2,1)S(1)} %get-tuple-element.137), kind=kOutput, calls=%fused_computation.87 | convolution fusion | flops 50364416 | bytes 25206784 | tf_op jit(solution)/shard_map/bcd,de->bce/dot_general | solution.py:69
  323.8 13.2 %all-gather = f32[2,12288]{1,0:T(2,128)S(1)} all-gather(f32[2,3072]{1,0:T(2,128)S(1)} %fusion.55), channel_id=2, replica_groups=mesh['dp'=8,'context'=4] {'context'}, dimensions={1}, use_global_device_ids=true | all-gather | bytes 122880 | tf_op jit(solution)/shard_map/all_gather | solution.py:70
  340.0 2.2 fusion.60
  342.3 5.6 %fusion.47 = (bf16[1,128,4096]{1,2,0:T(8,128)(2,1)}, bf16[1,128,4096]{1,2,0:T(8,128)(2,1)}) fusion(bf16[1,128,4096]{1,2,0:T(8,128)(2,1)S(1)} %copy-done.1, f32[1,128,32,128]{1,3,2,0:T(8,128)S(1)} %copy-done, f32[1,128,32,128]{1,3,2,0:T(8,128)S(1)} %copy.71, bf16[1,128,4096]{1,2,0:T(8,128)(2,1)S(1)} %copy.51, f32[4096]{0:T(1024)S(1)} %bitcast.203, ...), kind=kLoop, calls=%fused_computation.56 | loop fusion | flops 11534336 | bytes 8488960 | tf_op jit(solution)/shard_map/convert_element_type | solution.py:59
  347.8 2.4 copy.77
  350.2 1.3 copy.76
  (82 shorter events, 28.3 us)
Async XLA Ops:
  7.2 1.2 copy-start.5
  7.2 2.5 copy-start.6
  7.2 306.6 %all-gather.3.cloned.1.call-start = ((), (), s32[]{:S(2)}) async-start(), calls=%async_computation.2 | async-start | bytes 28311552 | tf_op jit(solution)/shard_map/all_gather | solution.py:68
  8.4 2.6 copy-start.7
  9.7 2.6 copy-start.8
  16.3 2.5 copy-start.4
  16.3 3.5 copy-start.3
  33.0 145.2 %all-to-all-start = ((bf16[6,128,32,128]{3,1,0,2:T(8,128)(2,1)}), bf16[6,128,32,128]{3,1,0,2:T(8,128)(2,1)}, u32[]{:S(2)}, u32[]{:S(2)}) async-start(bf16[6,128,32,128]{3,1,0,2:T(8,128)(2,1)} %copy.58), calls=%async_computation | async-start | bytes 12582912 | tf_op jit(solution)/shard_map/all_to_all | solution.py:95
  256.1 51.5 %all-to-all-start.1 = ((bf16[2,8,512,128]{3,1,0,2:T(8,128)(2,1)}), bf16[2,8,512,128]{3,1,0,2:T(8,128)(2,1)S(1)}, u32[]{:S(2)}, u32[]{:S(2)}) async-start(bf16[2,8,512,128]{3,1,0,2:T(8,128)(2,1)} %pad_maximum_fusion), calls=%async_computation.1 | async-start | bytes 4194304 | tf_op jit(solution)/shard_map/all_to_all | solution.py:102
  260.0 3.9 %copy-start.10 = (f32[1,4096]{1,0:T(1,128)S(1)}, f32[1,4096]{1,0:T(1,128)}, u32[]{:S(2)}) copy-start(f32[1,4096]{1,0:T(1,128)} %param.22) | copy-start | bytes 49156
  260.0 4.0 %copy-start.11 = (f32[1,4096]{1,0:T(1,128)S(1)}, f32[1,4096]{1,0:T(1,128)}, u32[]{:S(2)}) copy-start(f32[1,4096]{1,0:T(1,128)} %param.23) | copy-start | bytes 49156
  313.8 23.3 %copy-start.9 = (f32[3,4096]{1,0:T(4,128)S(1)}, f32[3,4096]{1,0:T(4,128)}, u32[]{:S(2)}) copy-start(f32[3,4096]{1,0:T(4,128)} %param.25) | copy-start | bytes 147460
  338.2 1.6 copy-start
  338.2 1.9 copy-start.1
  347.8 2.4 copy-start.2
Sparse Core Ops, SparseCore 0:
  9.9 128.0 all-gather.2
where the time goes:
time: 360 us; the launch traced here: 358 us
  waiting for transfers between devices  183 us (51%)
  matrix products  66.2 us (18%)
  local copies, waits for them, and re-layouts  54.8 us (15%)
  other arithmetic  16.1 us (4%)
  between operations  14.3 us (4%)
  blocking collectives  13.2 us (4%)
  starting transfers between devices  10.2 us (3%)
    all_to_all x1, waiting for transfers between devices, on_device(): lax.all_to_all(stacked, 'context', split_axis=2, concat_axis=1, tiled=True)  139 us
    all_to_all x1, waiting for transfers between devices, on_device(): lax.all_to_all(joined, 'context', split_axis=2, concat_axis=1, tiled=True)  43.6 us
    unnamed x39, local copies, waits for them, and re-layouts  23.5 us
    all_gather x1, blocking collectives, time_modulation(): whole = lax.all_gather(local, 'context', axis=2, tiled=True)  13.2 us
    dot_general x8, matrix products, one_block(): jnp.dot(block_q, key_dot.T, preferred_element_type=jnp.float32)  11.1 us
    another operation x2, local copies, waits for them, and re-layouts, on_device(): jnp.stack([source[0].reshape(tokens_dev, HEADS, HEAD) for source in sourc...  10 us
    dot_general x1, matrix products, time_modulation(): jnp.einsum('bcd,de->bce', both, full_rows, preferred_element_type=jnp.flo...  9.93 us
    dot_general x8, matrix products, one_block(): jnp.dot(probs_low, value_dot, preferred_element_type=jnp.float32)  9.9 us
  transfers between devices with their start and end apart: 3, of which 2 were waited for; matrix products, arithmetic and copies ran while one was open for 31% of the time, Pallas kernels for 0%

commit v1 on v0

v1 whole, which is shorter than its diff:
```python
import functools
import math

import jax
import jax.numpy as jnp
from jax import lax
from jax.experimental import pallas as pl
from jax.experimental.pallas import tpu as pltpu
from jax.sharding import PartitionSpec as P

HEADS = 32
HEAD = 128
EPS = 1e-06
MESH = pl.DeviceIdType.MESH


def flip(index, mask):
    bit = 1
    while bit <= mask:
        if mask & bit:
            index = index + bit * (1 - 2 * lax.rem(index // bit, 2))
        bit *= 2
    return index


def kernel(
    n_ctx,
    n_dp,
    res_ref,
    rest_ref,
    q_ref,
    k_ref,
    v_ref,
    dq_ref,
    dk_ref,
    dv_ref,
    tf_ref,
    tt_ref,
    w_ref,
    bm_ref,
    out_ref,
    outt_ref,
    rbuf,
    obuf,
    ret,
    resv,
    wv,
    act_s,
    act_r,
    part_s,
    part_r,
    mod_s,
    mod_r,
    mods,
    outv,
    in_send,
    in_recv,
    own_sem,
    ret_send,
    ret_recv,
    act_send,
    act_recv,
    part_send,
    part_recv,
    mod_send,
    mod_recv,
    loc_sem,
    out_sem,
):
    heads, _, length, _ = rbuf.shape
    tokens = ret.shape[1]
    width = ret.shape[2]
    rows_w, cols_w = wv.shape
    me = lax.axis_index("context")
    clip = lax.axis_index("dp")
    masks = list(range(n_ctx - 1, 0, -1))
    steps = list(range(1, n_dp))
    sources = (q_ref, k_ref, v_ref, dq_ref, dk_ref, dv_ref)

    barrier = pltpu.get_barrier_semaphore()
    for mask in masks:
        pl.semaphore_signal(barrier, inc=1, device_id={"context": flip(me, mask)}, device_id_type=MESH)
    for step in steps:
        pl.semaphore_signal(barrier, inc=1, device_id={"dp": lax.rem(clip + step, n_dp)}, device_id_type=MESH)

    local = [
        pltpu.make_async_copy(w_ref, wv, loc_sem.at[0]),
        pltpu.make_async_copy(res_ref.at[0], resv.at[0], loc_sem.at[1]),
        pltpu.make_async_copy(rest_ref.at[0], resv.at[1], loc_sem.at[2]),
    ]
    local[0].start()

    def own_rows(owner):
        return pl.ds(pl.multiple_of(owner * tokens, tokens), tokens)

    mine = own_rows(me)
    pl.semaphore_wait(barrier, len(masks) + len(steps))

    def send_head(head, carry):
        for mask in masks:
            peer = flip(me, mask)
            at = pl.multiple_of((peer * heads + head) * HEAD, HEAD)
            for slot, source in enumerate(sources):
                pltpu.make_async_remote_copy(
                    src_ref=source.at[0, :, pl.ds(at, HEAD)],
                    dst_ref=rbuf.at[head, slot, mine, :],
                    send_sem=in_send.at[mask - 1],
                    recv_sem=in_recv.at[head, mask - 1],
                    device_id={"context": peer},
                    device_id_type=MESH,
                ).start()
        return carry

    lax.fori_loop(0, heads, send_head, 0)

    def own_head(head, carry):
        at = pl.multiple_of((me * heads + head) * HEAD, HEAD)
        for slot, source in enumerate(sources):
            pltpu.make_async_copy(
                source.at[0, :, pl.ds(at, HEAD)], rbuf.at[head, slot, mine, :], own_sem.at[head]
            ).start()
        return carry

    x = tf_ref[...]
    gate = 1.0 / (1.0 + jnp.exp(-x))
    act = x * gate
    act_dot = tt_ref[...] * (gate * (1.0 + x * (1.0 - gate)))
    act_s[...] = jnp.zeros_like(act_s)
    for step in range(n_dp):
        act_s[step, 0:1, :] = act[:, step * rows_w : (step + 1) * rows_w]
        act_s[step, 1:2, :] = act_dot[:, step * rows_w : (step + 1) * rows_w]
    act_copies = []
    for step in steps:
        peer = lax.rem(clip + step, n_dp)
        copy = pltpu.make_async_remote_copy(
            src_ref=act_s.at[peer],
            dst_ref=act_r.at[clip],
            send_sem=act_send.at[step - 1],
            recv_sem=act_recv.at[step - 1],
            device_id={"dp": peer},
            device_id_type=MESH,
        )
        copy.start()
        act_copies.append(copy)
    lax.fori_loop(0, heads, own_head, 0)
    local[1].start()
    local[2].start()
    act_r[clip] = act_s[clip]
    for copy in act_copies:
        copy.wait()
    local[0].wait()
    lhs = act_r[...].reshape(n_dp * 8, rows_w).astype(jnp.bfloat16)
    tile = cols_w // 6

    for t in range(6):
        cols = slice(t * tile, (t + 1) * tile)
        prod = jnp.dot(lhs, wv[:, cols], preferred_element_type=jnp.float32)
        part_s[:, :, cols] = prod.reshape(n_dp, 8, tile)
    part_copies = []
    for step in steps:
        peer = lax.rem(clip + step, n_dp)
        copy = pltpu.make_async_remote_copy(
            src_ref=part_s.at[peer],
            dst_ref=part_r.at[clip],
            send_sem=part_send.at[step - 1],
            recv_sem=part_recv.at[step - 1],
            device_id={"dp": peer},
            device_id_type=MESH,
        )
        copy.start()
        part_copies.append(copy)
    part_r[clip] = part_s[clip]
    for copy in part_copies:
        copy.wait()
    total = part_r[0]
    for step in steps:
        total = total + part_r[step]
    quarter = cols_w // 4
    for piece in range(4):
        mod_s[2 * piece : 2 * piece + 2, :] = total[0:2, piece * quarter : (piece + 1) * quarter]
    mod_copies = []
    for mask in masks:
        copy = pltpu.make_async_remote_copy(
            src_ref=mod_s,
            dst_ref=mod_r.at[me],
            send_sem=mod_send.at[mask - 1],
            recv_sem=mod_recv.at[mask - 1],
            device_id={"context": flip(me, mask)},
            device_id_type=MESH,
        )
        copy.start()
        mod_copies.append(copy)
    mod_r[me] = mod_s[...]

    factor = 1.0 / HEAD**0.5
    block = min(256, length)

    def one_head(head, carry):
        pltpu.make_async_copy(rbuf.at[head, :, mine, :], rbuf.at[head, :, mine, :], own_sem.at[head]).wait()
        for mask in masks:
            theirs = rbuf.at[head, :, own_rows(flip(me, mask)), :]
            pltpu.make_async_copy(theirs, theirs, in_recv.at[head, mask - 1]).wait()

        def one_block(index, carry):
            rows = pl.ds(pl.multiple_of(index * block, block), block)
            query = rbuf[head, 0, rows, :]
            query_dot = rbuf[head, 3, rows, :]
            keyset = rbuf[head, 1]
            key_dot = rbuf[head, 4]
            values = rbuf[head, 2]
            value_dot = rbuf[head, 5]
            last = (((1,), (1,)), ((), ()))
            scores = lax.dot_general(query, keyset, last, preferred_element_type=jnp.float32) * factor
            score_dot = (
                lax.dot_general(
                    jnp.concatenate([query_dot, query], axis=1),
                    jnp.concatenate([keyset, key_dot], axis=1),
                    last,
                    preferred_element_type=jnp.float32,
                )
                * factor
            )
            top = jnp.max(scores, axis=1, keepdims=True)
            expo = jnp.exp(scores - top)
            probs = expo * (1.0 / jnp.sum(expo, axis=1, keepdims=True))
            probs_low = probs.astype(jnp.bfloat16)
            weighted = probs * score_dot
            centre = jnp.sum(weighted, axis=1, keepdims=True)
            weighted_low = weighted.astype(jnp.bfloat16)
            both = jnp.dot(
                probs_low, jnp.concatenate([values, value_dot], axis=1), preferred_element_type=jnp.float32
            )
            attended = both[:, :HEAD]
            tangent = (
                both[:, HEAD:]
                + jnp.dot(weighted_low, values, preferred_element_type=jnp.float32)
                - centre * attended
            )
            obuf[head, 0, rows, :] = attended.astype(jnp.bfloat16)
            obuf[head, 1, rows, :] = tangent.astype(jnp.bfloat16)
            return carry

        lax.fori_loop(0, length // block, one_block, 0)
        columns = pl.ds(pl.multiple_of((me * heads + head) * HEAD, HEAD), HEAD)
        for mask in masks:
            peer = flip(me, mask)
            pltpu.make_async_remote_copy(
                src_ref=obuf.at[head, :, own_rows(peer), :],
                dst_ref=ret.at[:, :, columns],
                send_sem=ret_send.at[mask - 1],
                recv_sem=ret_recv.at[mask - 1],
                device_id={"context": peer},
                device_id_type=MESH,
            ).start()
        ret[:, :, columns] = obuf[head, :, mine, :]
        return carry

    lax.fori_loop(0, heads, one_head, 0)

    for copy in mod_copies:
        copy.wait()
    chunk = math.gcd(quarter, width)
    for piece in range(3 * width // chunk):
        row, at = divmod(piece * chunk, width)
        owner, inside = divmod(piece * chunk, cols_w)
        part, off = divmod(inside, quarter)
        mods[row : row + 1, at : at + chunk] = (
            mod_r[owner, 2 * part : 2 * part + 1, off : off + chunk] + bm_ref[row : row + 1, at : at + chunk]
        )
        mods[row + 3 : row + 4, at : at + chunk] = mod_r[owner, 2 * part + 1 : 2 * part + 2, off : off + chunk]
    local[1].wait()
    local[2].wait()
    mods[2:3, :] = 1.0 + mods[2:3, :]

    for mask in masks:
        columns = pl.ds(pl.multiple_of(flip(me, mask) * (heads * HEAD), HEAD), heads * HEAD)
        theirs = ret.at[:, :, columns]
        pltpu.make_async_copy(theirs, theirs, ret_recv.at[mask - 1]).wait()

    lines = 16

    def norm(index, carry):
        rows = pl.ds(pl.multiple_of(index * lines, lines), lines)
        att = ret[0, rows, :].astype(jnp.float32)
        hidden = resv[0, rows, :].astype(jnp.float32) + mods[0:1, :] * att
        hidden_dot = (
            resv[1, rows, :].astype(jnp.float32)
            + mods[0:1, :] * ret[1, rows, :].astype(jnp.float32)
            + mods[3:4, :] * att
        )
        centered = hidden - jnp.mean(hidden, axis=1, keepdims=True)
        inverse = lax.rsqrt(jnp.mean(centered * centered, axis=1, keepdims=True) + EPS)
        unit = centered * inverse
        unit_dot = (
            hidden_dot
            - jnp.mean(hidden_dot, axis=1, keepdims=True)
            - unit * jnp.mean(unit * hidden_dot, axis=1, keepdims=True)
        ) * inverse
        outv[0, rows, :] = (unit * mods[2:3, :] + mods[1:2, :]).astype(jnp.bfloat16)
        outv[1, rows, :] = (unit_dot * mods[2:3, :] + unit * mods[5:6, :] + mods[4:5, :]).astype(jnp.bfloat16)
        pltpu.make_async_copy(outv.at[0, rows, :], out_ref.at[0, rows, :], out_sem.at[0]).start()
        pltpu.make_async_copy(outv.at[1, rows, :], outt_ref.at[0, rows, :], out_sem.at[1]).start()
        return carry

    lax.fori_loop(0, tokens // lines, norm, 0)

    for mask in masks:
        sent = rbuf.at[:, :, mine, :]
        pltpu.make_async_copy(sent, sent, in_send.at[mask - 1]).wait()
        sent = obuf.at[:, :, mine, :]
        pltpu.make_async_copy(sent, sent, ret_send.at[mask - 1]).wait()
    pltpu.make_async_copy(outv.at[0], out_ref.at[0], out_sem.at[0]).wait()
    pltpu.make_async_copy(outv.at[1], outt_ref.at[0], out_sem.at[1]).wait()


def on_device(n_ctx, n_dp, *arrays):
    res, q, tf, w = arrays[0], arrays[2], arrays[8], arrays[10]
    _, tokens, width = res.shape
    length = tokens * n_ctx
    heads = HEADS // n_ctx
    rows_w, cols_w = w.shape
    bf16, f32 = jnp.bfloat16, jnp.float32
    dma = pltpu.SemaphoreType.DMA
    anywhere = pl.BlockSpec(memory_space=pl.ANY)
    vmem = pl.BlockSpec(memory_space=pltpu.VMEM)
    return pl.pallas_call(
        functools.partial(kernel, n_ctx, n_dp),
        out_shape=(jax.ShapeDtypeStruct(res.shape, bf16),) * 2,
        in_specs=[anywhere] * 8 + [vmem, vmem, anywhere, vmem],
        out_specs=(anywhere,) * 2,
        scratch_shapes=[
            pltpu.VMEM((heads, 6, length, HEAD), bf16),
            pltpu.VMEM((heads, 2, length, HEAD), bf16),
            pltpu.VMEM((2, tokens, width), bf16),
            pltpu.VMEM((2, tokens, width), bf16),
            pltpu.VMEM((rows_w, cols_w), bf16),
            pltpu.VMEM((n_dp, 8, rows_w), f32),
            pltpu.VMEM((n_dp, 8, rows_w), f32),
            pltpu.VMEM((n_dp, 8, cols_w), f32),
            pltpu.VMEM((n_dp, 8, cols_w), f32),
            pltpu.VMEM((8, cols_w // 4), f32),
            pltpu.VMEM((n_ctx, 8, cols_w // 4), f32),
            pltpu.VMEM((8, width), f32),
            pltpu.VMEM((2, tokens, width), bf16),
            dma((n_ctx - 1,)),
            dma((heads, n_ctx - 1)),
            dma((heads,)),
            dma((n_ctx - 1,)),
            dma((n_ctx - 1,)),
            dma((n_dp - 1,)),
            dma((n_dp - 1,)),
            dma((n_dp - 1,)),
            dma((n_dp - 1,)),
            dma((n_ctx - 1,)),
            dma((n_ctx - 1,)),
            dma((3,)),
            dma((2,)),
        ],
        compiler_params=pltpu.CompilerParams(
            collective_id=0, has_side_effects=True, vmem_limit_bytes=56 * 1024 * 1024
        ),
    )(*arrays)


def solution(mesh):
    spec = P("dp", "context", None)
    return jax.shard_map(
        functools.partial(on_device, mesh.shape["context"], mesh.shape["dp"]),
        mesh=mesh,
        in_specs=(spec,) * 8 + (P("dp", None), P("dp", None), P("dp", "context"), P()),
        out_specs=(spec, spec),
        check_vma=False,
    )
```

time: 360 us -> 202 us (0.56)
  Pallas kernels: 0 us -> 196 us
  waiting for transfers between devices: 183 us -> 0 us
  matrix products: 66.2 us -> 0 us
  local copies, waits for them, and re-layouts: 54.8 us -> 4.57 us
  other arithmetic: 16.1 us -> 0 us
  between operations: 14.3 us -> 0.64 us
  blocking collectives: 13.2 us -> 0 us
  starting transfers between devices: 10.2 us -> 0 us
    pallas_call x0 -> x1, Pallas kernels: none -> 196 us  [on_device(): pl.pallas_call(functools.partial(kernel, n_ctx, n_dp), out_shape=(jax.Sha...]
    all_to_all x2 -> x0, waiting for transfers between devices: 183 us -> none  [the longest x1 139 us: on_device(): lax.all_to_all(stacked, 'context', split_axis=2, concat_axis=1, tiled=True)]
    dot_general x49 -> x0, matrix products: 66.2 us -> none  [the longest x8 11.1 us: one_block(): jnp.dot(block_q, key_dot.T, preferred_element_type=jnp.float32)]
    unnamed x39 -> x2, local copies, waits for them, and re-layouts: 23.5 us -> 4.57 us
    all_gather x1 -> x0, blocking collectives: 13.2 us -> none  [time_modulation(): whole = lax.all_gather(local, 'context', axis=2, tiled=True)]
    another operation x4 -> x0, local copies, waits for them, and re-layouts: 12.9 us -> none  [the longest x2 10 us: on_device(): jnp.stack([source[0].reshape(tokens_dev, HEADS, HEAD) for source in sourc...]
    all_to_all x2 -> x0, starting transfers between devices: 10.1 us -> none  [the longest x1 6.32 us: on_device(): lax.all_to_all(stacked, 'context', split_axis=2, concat_axis=1, tiled=True)]
    all_to_all x2 -> x0, local copies, waits for them, and re-layouts: 9.06 us -> none  [the longest x1 8.52 us: on_device(): lax.all_to_all(stacked, 'context', split_axis=2, concat_axis=1, tiled=True)]
  transfers between devices with their start and end apart: 3 -> 0, of which waited for: 2 -> 0; matrix products, arithmetic and copies ran while one was open for 31% -> 0% of each run, Pallas kernels for 0% -> 0%
where the time goes in v1:
time: 202 us; the launch traced here: 201 us
  Pallas kernels  196 us (97%)
  local copies, waits for them, and re-layouts  4.57 us (2%)
    pallas_call x1, Pallas kernels, on_device(): pl.pallas_call(functools.partial(kernel, n_ctx, n_dp), out_shape=(jax.Sha...  196 us
    unnamed x2, local copies, waits for them, and re-layouts  4.57 us

profile of v1, /device:TPU:0, one launch (start us, length us, event | category | flops | bytes accessed | tf_op | source)
XLA Modules:
  0.0 201.3 jit_solution(18247180645637631524)
XLA Ops:
  0.6 196.1 %shard_map.131 = (bf16[1,128,4096]{2,1,0:T(8,128)(2,1)}, bf16[1,128,4096]{2,1,0:T(8,128)(2,1)}) custom-call(bf16[1,128,4096]{2,1,0:T(8,128)(2,1)} %res_ref.1, bf16[1,128,4096]{2,1,0:T(8,128)(2,1)} %rest_ref.1, bf16[1,128,4096]{2,1,0:T(8,128)(2,1)} %q_ref.1, bf16[1,128,4096]{2,1,0:T(8,128)(2,1)} %k_ref.1, bf16[1,128,4096]{2,1,0:T(8,128)(2,1)} %v_ref.1, ...), custom_call_target="tpu_custom_call" | custom-call | tf_op jit(solution)/shard_map/pallas_call | solution.py:326
  196.8 2.3 %copy.16 = bf16[1,128,4096]{2,1,0:T(8,128)(2,1)} copy(bf16[1,128,4096]{2,1,0:T(8,128)(2,1)} %get-tuple-element.4) | data formatting | bytes 2097152
  199.1 2.3 %copy.17 = bf16[1,128,4096]{2,1,0:T(8,128)(2,1)} copy(bf16[1,128,4096]{2,1,0:T(8,128)(2,1)} %get-tuple-element.5) | data formatting | bytes 2097152

commit v2 on v1

--- a/solution.py
+++ b/solution.py
@@ -11,6 +11,7 @@
 HEADS = 32
 HEAD = 128
 EPS = 1e-06
+BLOCK = 32
 MESH = pl.DeviceIdType.MESH
 
 
@@ -52,12 +53,13 @@
     mod_s,
     mod_r,
     mods,
-    outv,
     in_send,
     in_recv,
     own_sem,
     ret_send,
     ret_recv,
+    late_send,
+    late_recv,
     act_send,
     act_recv,
     part_send,
@@ -65,9 +67,9 @@
     mod_send,
     mod_recv,
     loc_sem,
-    out_sem,
 ):
     heads, _, length, _ = rbuf.shape
+    early = heads // 2
     tokens = ret.shape[1]
     width = ret.shape[2]
     rows_w, cols_w = wv.shape
@@ -201,6 +203,8 @@
             theirs = rbuf.at[head, :, own_rows(flip(me, mask)), :]
             pltpu.make_async_copy(theirs, theirs, in_recv.at[head, mask - 1]).wait()
 
+        here = pl.ds(pl.multiple_of(head * HEAD, HEAD), HEAD)
+
         def one_block(index, carry):
             rows = pl.ds(pl.multiple_of(index * block, block), block)
             query = rbuf[head, 0, rows, :]
@@ -236,26 +240,50 @@
                 + jnp.dot(weighted_low, values, preferred_element_type=jnp.float32)
                 - centre * attended
             )
-            obuf[head, 0, rows, :] = attended.astype(jnp.bfloat16)
-            obuf[head, 1, rows, :] = tangent.astype(jnp.bfloat16)
+            obuf[0, rows, here] = attended.astype(jnp.bfloat16)
+            obuf[1, rows, here] = tangent.astype(jnp.bfloat16)
             return carry
 
         lax.fori_loop(0, length // block, one_block, 0)
         columns = pl.ds(pl.multiple_of((me * heads + head) * HEAD, HEAD), HEAD)
+
+        @pl.when(head < early)
+        def _():
+            for mask in masks:
+                peer = flip(me, mask)
+                pltpu.make_async_remote_copy(
+                    src_ref=obuf.at[:, own_rows(peer), here],
+                    dst_ref=ret.at[:, :, columns],
+                    send_sem=ret_send.at[mask - 1],
+                    recv_sem=ret_recv.at[mask - 1],
+                    device_id={"context": peer},
+                    device_id_type=MESH,
+                ).start()
+
+        ret[:, :, columns] = obuf[:, mine, here]
+        return carry
+
+    lax.fori_loop(0, heads, one_head, 0)
+
+    span = (heads - early) * HEAD
+    late = pl.ds(early * HEAD, span)
+    late_out = pl.ds(pl.multiple_of((me * heads + early) * HEAD, HEAD), span)
+    blocks = tokens // BLOCK
+
+    def send_block(index, carry):
         for mask in masks:
             peer = flip(me, mask)
             pltpu.make_async_remote_copy(
-                src_ref=obuf.at[head, :, own_rows(peer), :],
-                dst_ref=ret.at[:, :, columns],
-                send_sem=ret_send.at[mask - 1],
-                recv_sem=ret_recv.at[mask - 1],
+                src_ref=obuf.at[:, pl.ds(pl.multiple_of(peer * tokens + index * BLOCK, BLOCK), BLOCK), late],
+                dst_ref=ret.at[:, pl.ds(pl.multiple_of(index * BLOCK, BLOCK), BLOCK), late_out],
+                send_sem=late_send.at[mask - 1],
+                recv_sem=late_recv.at[index, mask - 1],
                 device_id={"context": peer},
                 device_id_type=MESH,
             ).start()
-        ret[:, :, columns] = obuf[head, :, mine, :]
-        return carry
-
-    lax.fori_loop(0, heads, one_head, 0)
+        return carry
+
+    lax.fori_loop(0, blocks, send_block, 0)
 
     for copy in mod_copies:
         copy.wait()
@@ -273,7 +301,7 @@
     mods[2:3, :] = 1.0 + mods[2:3, :]
 
     for mask in masks:
-        columns = pl.ds(pl.multiple_of(flip(me, mask) * (heads * HEAD), HEAD), heads * HEAD)
+        columns = pl.ds(pl.multiple_of(flip(me, mask) * (heads * HEAD), HEAD), early * HEAD)
         theirs = ret.at[:, :, columns]
         pltpu.make_async_copy(theirs, theirs, ret_recv.at[mask - 1]).wait()
 
@@ -296,21 +324,27 @@
             - jnp.mean(hidden_dot, axis=1, keepdims=True)
             - unit * jnp.mean(unit * hidden_dot, axis=1, keepdims=True)
         ) * inverse
-        outv[0, rows, :] = (unit * mods[2:3, :] + mods[1:2, :]).astype(jnp.bfloat16)
-        outv[1, rows, :] = (unit_dot * mods[2:3, :] + unit * mods[5:6, :] + mods[4:5, :]).astype(jnp.bfloat16)
-        pltpu.make_async_copy(outv.at[0, rows, :], out_ref.at[0, rows, :], out_sem.at[0]).start()
-        pltpu.make_async_copy(outv.at[1, rows, :], outt_ref.at[0, rows, :], out_sem.at[1]).start()
-        return carry
-
-    lax.fori_loop(0, tokens // lines, norm, 0)
+        out_ref[0, rows, :] = (unit * mods[2:3, :] + mods[1:2, :]).astype(jnp.bfloat16)
+        outt_ref[0, rows, :] = (unit_dot * mods[2:3, :] + unit * mods[5:6, :] + mods[4:5, :]).astype(jnp.bfloat16)
+        return carry
+
+    def norm_block(index, carry):
+        for mask in masks:
+            columns = pl.ds(pl.multiple_of((flip(me, mask) * heads + early) * HEAD, HEAD), span)
+            theirs = ret.at[:, pl.ds(pl.multiple_of(index * BLOCK, BLOCK), BLOCK), columns]
+            pltpu.make_async_copy(theirs, theirs, late_recv.at[index, mask - 1]).wait()
+        lax.fori_loop(index * (BLOCK // lines), (index + 1) * (BLOCK // lines), norm, 0)
+        return carry
+
+    lax.fori_loop(0, blocks, norm_block, 0)
 
     for mask in masks:
         sent = rbuf.at[:, :, mine, :]
         pltpu.make_async_copy(sent, sent, in_send.at[mask - 1]).wait()
-        sent = obuf.at[:, :, mine, :]
+        sent = obuf.at[:, mine, pl.ds(0, early * HEAD)]
         pltpu.make_async_copy(sent, sent, ret_send.at[mask - 1]).wait()
-    pltpu.make_async_copy(outv.at[0], out_ref.at[0], out_sem.at[0]).wait()
-    pltpu.make_async_copy(outv.at[1], outt_ref.at[0], out_sem.at[1]).wait()
+        sent = obuf.at[:, mine, late]
+        pltpu.make_async_copy(sent, sent, late_send.at[mask - 1]).wait()
 
 
 def on_device(n_ctx, n_dp, *arrays):
@@ -327,10 +361,10 @@
         functools.partial(kernel, n_ctx, n_dp),
         out_shape=(jax.ShapeDtypeStruct(res.shape, bf16),) * 2,
         in_specs=[anywhere] * 8 + [vmem, vmem, anywhere, vmem],
-        out_specs=(anywhere,) * 2,
+        out_specs=(vmem,) * 2,
         scratch_shapes=[
             pltpu.VMEM((heads, 6, length, HEAD), bf16),
-            pltpu.VMEM((heads, 2, length, HEAD), bf16),
+            pltpu.VMEM((2, length, heads * HEAD), bf16),
             pltpu.VMEM((2, tokens, width), bf16),
             pltpu.VMEM((2, tokens, width), bf16),
             pltpu.VMEM((rows_w, cols_w), bf16),
@@ -341,12 +375,13 @@
             pltpu.VMEM((8, cols_w // 4), f32),
             pltpu.VMEM((n_ctx, 8, cols_w // 4), f32),
             pltpu.VMEM((8, width), f32),
-            pltpu.VMEM((2, tokens, width), bf16),
             dma((n_ctx - 1,)),
             dma((heads, n_ctx - 1)),
             dma((heads,)),
             dma((n_ctx - 1,)),
             dma((n_ctx - 1,)),
+            dma((n_ctx - 1,)),
+            dma((tokens // BLOCK, n_ctx - 1)),
             dma((n_dp - 1,)),
             dma((n_dp - 1,)),
             dma((n_dp - 1,)),
@@ -354,12 +389,11 @@
             dma((n_ctx - 1,)),
             dma((n_ctx - 1,)),
             dma((3,)),
-            dma((2,)),
         ],
         compiler_params=pltpu.CompilerParams(
-            collective_id=0, has_side_effects=True, vmem_limit_bytes=56 * 1024 * 1024
+            collective_id=0, has_side_effects=True, vmem_limit_bytes=40 * 1024 * 1024
         ),
-    )(*arrays)
+    )(*(pltpu.with_memory_space_constraint(a, pltpu.HBM) for a in arrays))
 
 
 def solution(mesh):

time: 202 us -> 195 us (0.965)
  Pallas kernels: 196 us -> 193 us
  local copies, waits for them, and re-layouts: 4.57 us -> 1.94 us
    pallas_call x1, Pallas kernels: 196 us -> 193 us  [on_device(): pl.pallas_call(functools.partial(kernel, n_ctx, n_dp), out_shape=(jax.Sha...]
    unnamed x2, local copies, waits for them, and re-layouts: 4.57 us -> 1.94 us
where the time goes in v2:
time: 195 us
  Pallas kernels  193 us (99%)
    pallas_call x1, Pallas kernels, on_device(): pl.pallas_call(functools.partial(kernel, n_ctx, n_dp), out_shape=(jax.Sha...  193 us

profile of v2, /device:TPU:0, one launch (start us, length us, event | category | flops | bytes accessed | tf_op | source)
XLA Modules:
  0.0 195.2 jit_solution(4706030207267137962)
XLA Ops:
  0.6 192.6 %shard_map.131 = (bf16[1,128,4096]{2,1,0:T(8,128)(2,1)S(1)}, bf16[1,128,4096]{2,1,0:T(8,128)(2,1)S(1)}) custom-call(bf16[1,128,4096]{2,1,0:T(8,128)(2,1)} %res_ref.1, bf16[1,128,4096]{2,1,0:T(8,128)(2,1)} %rest_ref.1, bf16[1,128,4096]{2,1,0:T(8,128)(2,1)} %q_ref.1, bf16[1,128,4096]{2,1,0:T(8,128)(2,1)} %k_ref.1, bf16[1,128,4096]{2,1,0:T(8,128)(2,1)} %v_ref.1, ...), custom_call_target="tpu_custom_call" | custom-call | tf_op jit(solution)/shard_map/pallas_call | solution.py:360
  193.2 1.0 copy.16
  194.2 1.0 copy.17
